TPU v7x, 128 devices: a whole 4x4x4 slice. The times are simulated.
128 devices in a mesh: dp: 8 (over y, core), fsdp: 16 (over z, x).
Axes of the slice: x: 4, y: 4, z: 4, core: 2. Of those that a mesh axis runs over, the one named last changes fastest.
Arguments:
- tokens: bfloat16 [100352, 768], P(('dp', 'fsdp')), may hold values from -6 to 6
- keep_mask: int32 [512, 196], P(('dp', 'fsdp')), may hold values from 0 to 1, as said below
- pairing: int32 [512], replicated, may hold values from 0 to 511, each once
- text_vectors: float32 [512, 512], P(('dp', 'fsdp')), may hold values from -6 to 6
- logit_scale: float32 [1], replicated, may hold values from 3 to 3.8
- w_qkv: float32 [768, 2304], P(('dp', 'fsdp')), may hold values from -0.21875 to 0.21875
- w_out: float32 [768, 768], P(('dp', 'fsdp')), may hold values from -1.75 to 1.75
- w_up: float32 [768, 3072], P(('dp', 'fsdp')), may hold values from -0.21875 to 0.21875
- w_down: float32 [3072, 768], P(('dp', 'fsdp')), may hold values from -0.109375 to 0.109375
- w_proj: float32 [768, 512], P(('dp', 'fsdp')), may hold values from -0.21875 to 0.21875
- gain_one: float32 [768], P(('dp', 'fsdp')), may hold values from 0.25 to 1.75
- shift_one: float32 [768], P(('dp', 'fsdp')), may hold values from -1.5 to 1.5
- gain_two: float32 [768], P(('dp', 'fsdp')), may hold values from 0.25 to 1.75
- shift_two: float32 [768], P(('dp', 'fsdp')), may hold values from -1.5 to 1.5
- gain_post: float32 [768], P(('dp', 'fsdp')), may hold values from 0.25 to 1.75
- shift_post: float32 [768], P(('dp', 'fsdp')), may hold values from -1.5 to 1.5
- pool_query: float32 [768], P(('dp', 'fsdp')), may hold values from -10 to 10
Outputs:
- loss_value: float32 [1], replicated
- grad_tokens: float32 [100352, 768], P(('dp', 'fsdp'))
- grad_text: float32 [512, 512], P(('dp', 'fsdp'))
- grad_qkv: float32 [768, 2304], P(('dp', 'fsdp'))
- grad_out: float32 [768, 768], P(('dp', 'fsdp'))
- grad_up: float32 [768, 3072], P(('dp', 'fsdp'))
- grad_down: float32 [3072, 768], P(('dp', 'fsdp'))
- grad_proj: float32 [768, 512], P(('dp', 'fsdp'))
- grad_gain_one: float32 [768], P(('dp', 'fsdp'))
- grad_shift_one: float32 [768], P(('dp', 'fsdp'))
- grad_gain_two: float32 [768], P(('dp', 'fsdp'))
- grad_shift_two: float32 [768], P(('dp', 'fsdp'))
- grad_gain_post: float32 [768], P(('dp', 'fsdp'))
- grad_shift_post: float32 [768], P(('dp', 'fsdp'))
- grad_query: float32 [768], P(('dp', 'fsdp'))
- grad_scale: float32 [1], replicated
Inputs may be any that keep to these rules, and one draw needn't show every extreme that they name: `keep_mask`: each image keeps between 32 and 196 patches; some image keeps all 196 and some exactly 32. `pairing`: each text row belongs to exactly one image.
All inputs are finite; a program needn't handle non-finite values.
Results may differ from a plain program's by a relative error of at most 0.022.
Values may be sent and summed in bfloat16 or wider, within the bound.
A program may use at most 192 MiB of HBM per device.

v0:
```python
from functools import partial
import math

import jax
import jax.numpy as jnp
from jax import lax
from jax.sharding import PartitionSpec as P

HEADS = 12
HDIM = 64


def norm_rows(values, norm_gain, norm_shift):
    center = jnp.mean(values, axis=-1, keepdims=True)
    centred = values - center
    spread = jnp.mean(centred * centred, axis=-1, keepdims=True)
    return centred * lax.rsqrt(spread + 1e-05) * norm_gain + norm_shift


def unit_rows(values):
    row_total = jnp.sum(values * values, axis=-1, keepdims=True) + 1e-06
    return values * lax.rsqrt(row_total)


def pooled_rows(residual_two, norm_gain, norm_shift, query_vec, kept_mask):
    images_here, patches = kept_mask.shape
    final = norm_rows(residual_two, norm_gain, norm_shift).reshape(images_here, patches, -1)
    pool_logits = jnp.sum(final * query_vec, axis=-1) / math.sqrt(final.shape[-1])
    pool_logits = jnp.where(kept_mask > 0, pool_logits, -1e30)
    shares = jax.nn.softmax(pool_logits, axis=-1)
    return jnp.sum(shares[:, :, None] * final, axis=1)


def head_loss(image_rows, text_rows, scale_log, pairing):
    total_rows = image_rows.shape[0]
    logits = jnp.exp(scale_log[0]) * jnp.dot(
        image_rows, text_rows.T, precision=lax.Precision.HIGHEST
    )
    target = (pairing[:, None] == jnp.arange(total_rows, dtype=jnp.int32)[None, :]).astype(
        logits.dtype
    )
    row_totals = jax.nn.logsumexp(logits, axis=1)
    col_totals = jax.nn.logsumexp(logits, axis=0)
    matched = jnp.sum(logits * target)
    return (jnp.sum(row_totals) + jnp.sum(col_totals) - 2.0 * matched) / (2.0 * total_rows)


def shards(
    tokens,
    keep_mask,
    pairing,
    text_vectors,
    logit_scale,
    w_qkv,
    w_out,
    w_up,
    w_down,
    w_proj,
    gain_one,
    shift_one,
    gain_two,
    shift_two,
    gain_post,
    shift_post,
    pool_query,
):
    gathered = (
        lax.all_gather(w_qkv.astype(jnp.bfloat16), ("dp", "fsdp"), axis=0, tiled=True),
        lax.all_gather(w_out.astype(jnp.bfloat16), ("dp", "fsdp"), axis=0, tiled=True),
        lax.all_gather(w_up.astype(jnp.bfloat16), ("dp", "fsdp"), axis=0, tiled=True),
        lax.all_gather(w_down.astype(jnp.bfloat16), ("dp", "fsdp"), axis=0, tiled=True),
        lax.all_gather(w_proj.astype(jnp.bfloat16), ("dp", "fsdp"), axis=0, tiled=True),
        lax.all_gather(gain_one.astype(jnp.bfloat16), ("dp", "fsdp"), axis=0, tiled=True),
        lax.all_gather(shift_one.astype(jnp.bfloat16), ("dp", "fsdp"), axis=0, tiled=True),
        lax.all_gather(gain_two.astype(jnp.bfloat16), ("dp", "fsdp"), axis=0, tiled=True),
        lax.all_gather(shift_two.astype(jnp.bfloat16), ("dp", "fsdp"), axis=0, tiled=True),
        lax.all_gather(gain_post.astype(jnp.bfloat16), ("dp", "fsdp"), axis=0, tiled=True),
        lax.all_gather(shift_post.astype(jnp.bfloat16), ("dp", "fsdp"), axis=0, tiled=True),
        lax.all_gather(pool_query.astype(jnp.bfloat16), ("dp", "fsdp"), axis=0, tiled=True),
    )
    qkv_full, out_full, up_full, down_full, proj_full = (
        gathered[0],
        gathered[1],
        gathered[2],
        gathered[3],
        gathered[4],
    )
    gain_first = gathered[5].astype(jnp.float32)
    shift_first = gathered[6].astype(jnp.float32)
    gain_second = gathered[7].astype(jnp.float32)
    shift_second = gathered[8].astype(jnp.float32)
    gain_last = gathered[9].astype(jnp.float32)
    shift_last = gathered[10].astype(jnp.float32)
    query_full = gathered[11].astype(jnp.float32)
    images_here, patches = keep_mask.shape
    model_width = tokens.shape[1]
    row_count = images_here * patches
    scaling = HDIM ** (-0.5)
    live_keys = (keep_mask > 0)[:, None, None, :]
    inputs = tokens.astype(jnp.float32)
    normed_one, norm_one_back = jax.vjp(norm_rows, inputs, gain_first, shift_first)
    normed = normed_one.astype(jnp.bfloat16)
    mixed = jnp.dot(normed, qkv_full, preferred_element_type=jnp.float32).astype(jnp.bfloat16)
    mixed = mixed.reshape(images_here, patches, 3, HEADS, HDIM)
    queries = mixed[:, :, 0]
    key_rows = mixed[:, :, 1]
    values = mixed[:, :, 2]
    raw_scores = (
        jnp.einsum("bqhd,bkhd->bhqk", queries, key_rows, preferred_element_type=jnp.float32)
        * scaling
    )
    raw_scores = jnp.where(live_keys, raw_scores, -1e30)
    log_total = jax.nn.logsumexp(raw_scores, axis=-1, keepdims=True)
    softmaxed = jnp.exp(raw_scores - log_total).astype(jnp.bfloat16)
    attended = jnp.einsum("bhqk,bkhd->bqhd", softmaxed, values, preferred_element_type=jnp.float32)
    attended = attended.astype(jnp.bfloat16).reshape(row_count, model_width)
    residual_one = inputs + jnp.dot(attended, out_full, preferred_element_type=jnp.float32)
    normed_mid, norm_two_back = jax.vjp(norm_rows, residual_one, gain_second, shift_second)
    normed_two = normed_mid.astype(jnp.bfloat16)
    upward = jnp.dot(normed_two, up_full, preferred_element_type=jnp.float32)
    active_full, gelu_back = jax.vjp(partial(jax.nn.gelu, approximate=False), upward)
    active = active_full.astype(jnp.bfloat16)
    residual_two = residual_one + jnp.dot(active, down_full, preferred_element_type=jnp.float32)
    pooled, pool_back = jax.vjp(
        partial(pooled_rows, kept_mask=keep_mask), residual_two, gain_last, shift_last, query_full
    )
    pooled_half = pooled.astype(jnp.bfloat16)
    embedded = jnp.dot(pooled_half, proj_full, preferred_element_type=jnp.float32)
    unit_image, unit_back = jax.vjp(unit_rows, embedded)
    unit_text, text_back = jax.vjp(unit_rows, text_vectors)
    image_all, text_all = (
        lax.all_gather(unit_image.astype(jnp.bfloat16), ("dp", "fsdp"), axis=0, tiled=True),
        lax.all_gather(unit_text.astype(jnp.bfloat16), ("dp", "fsdp"), axis=0, tiled=True),
    )
    loss_value, head_back = jax.vjp(
        partial(head_loss, pairing=pairing),
        image_all.astype(jnp.float32),
        text_all.astype(jnp.float32),
        logit_scale,
    )
    grad_image_all, grad_text_all, grad_scale = head_back(jnp.ones_like(loss_value))
    offset = lax.axis_index(("dp", "fsdp")) * images_here
    grad_unit = lax.dynamic_slice_in_dim(grad_image_all, offset, images_here, 0)
    grad_unit_text = lax.dynamic_slice_in_dim(grad_text_all, offset, images_here, 0)
    grad_text = text_back(grad_unit_text)[0]
    grad_embed = unit_back(grad_unit)[0].astype(jnp.bfloat16)
    qkv_back, out_back, up_back, down_back, proj_back = (
        lax.all_gather(w_qkv.astype(jnp.bfloat16), ("dp", "fsdp"), axis=0, tiled=True),
        lax.all_gather(w_out.astype(jnp.bfloat16), ("dp", "fsdp"), axis=0, tiled=True),
        lax.all_gather(w_up.astype(jnp.bfloat16), ("dp", "fsdp"), axis=0, tiled=True),
        lax.all_gather(w_down.astype(jnp.bfloat16), ("dp", "fsdp"), axis=0, tiled=True),
        lax.all_gather(w_proj.astype(jnp.bfloat16), ("dp", "fsdp"), axis=0, tiled=True),
    )
    grad_proj = jnp.dot(pooled_half.T, grad_embed, preferred_element_type=jnp.float32)
    grad_pooled = jnp.dot(grad_embed, proj_back.T, preferred_element_type=jnp.float32)
    grad_second, grad_gain_post, grad_shift_post, grad_query = pool_back(grad_pooled)
    grad_branch_two = grad_second.astype(jnp.bfloat16)
    grad_down = jnp.dot(active.T, grad_branch_two, preferred_element_type=jnp.float32)
    grad_active = jnp.dot(grad_branch_two, down_back.T, preferred_element_type=jnp.float32)
    grad_upward = gelu_back(grad_active)[0].astype(jnp.bfloat16)
    grad_up = jnp.dot(normed_two.T, grad_upward, preferred_element_type=jnp.float32)
    grad_normed_two = jnp.dot(grad_upward, up_back.T, preferred_element_type=jnp.float32)
    grad_first_norm, grad_gain_two, grad_shift_two = norm_two_back(grad_normed_two)
    grad_first = grad_second + grad_first_norm
    grad_branch = grad_first.astype(jnp.bfloat16)
    grad_out = jnp.dot(attended.T, grad_branch, preferred_element_type=jnp.float32)
    grad_attended = jnp.dot(grad_branch, out_back.T, preferred_element_type=jnp.float32)
    grad_attended = grad_attended.astype(jnp.bfloat16).reshape(images_here, patches, HEADS, HDIM)
    again_scores = (
        jnp.einsum("bqhd,bkhd->bhqk", queries, key_rows, preferred_element_type=jnp.float32)
        * scaling
    )
    again_scores = jnp.where(live_keys, again_scores, -1e30)
    probs_again = jnp.exp(again_scores - log_total)
    grad_probs = jnp.einsum(
        "bqhd,bkhd->bhqk", grad_attended, values, preferred_element_type=jnp.float32
    )
    grad_values = jnp.einsum(
        "bhqk,bqhd->bkhd",
        probs_again.astype(jnp.bfloat16),
        grad_attended,
        preferred_element_type=jnp.float32,
    )
    grad_scores = probs_again * (
        grad_probs - jnp.sum(probs_again * grad_probs, axis=-1, keepdims=True)
    )
    grad_scores = grad_scores.astype(jnp.bfloat16)
    grad_queries = (
        jnp.einsum("bhqk,bkhd->bqhd", grad_scores, key_rows, preferred_element_type=jnp.float32)
        * scaling
    )
    grad_keys = (
        jnp.einsum("bhqk,bqhd->bkhd", grad_scores, queries, preferred_element_type=jnp.float32)
        * scaling
    )
    grad_mixed = jnp.stack([grad_queries, grad_keys, grad_values], axis=2).astype(jnp.bfloat16)
    grad_mixed = grad_mixed.reshape(row_count, 3 * model_width)
    grad_qkv = jnp.dot(normed.T, grad_mixed, preferred_element_type=jnp.float32)
    grad_normed = jnp.dot(grad_mixed, qkv_back.T, preferred_element_type=jnp.float32)
    grad_input_norm, grad_gain_one, grad_shift_one = norm_one_back(grad_normed)
    grad_tokens = grad_first + grad_input_norm
    owned = (
        lax.psum_scatter(grad_qkv, ("dp", "fsdp"), scatter_dimension=0, tiled=True),
        lax.psum_scatter(grad_out, ("dp", "fsdp"), scatter_dimension=0, tiled=True),
        lax.psum_scatter(grad_up, ("dp", "fsdp"), scatter_dimension=0, tiled=True),
        lax.psum_scatter(grad_down, ("dp", "fsdp"), scatter_dimension=0, tiled=True),
        lax.psum_scatter(grad_proj, ("dp", "fsdp"), scatter_dimension=0, tiled=True),
        lax.psum_scatter(grad_gain_one, ("dp", "fsdp"), scatter_dimension=0, tiled=True),
        lax.psum_scatter(grad_shift_one, ("dp", "fsdp"), scatter_dimension=0, tiled=True),
        lax.psum_scatter(grad_gain_two, ("dp", "fsdp"), scatter_dimension=0, tiled=True),
        lax.psum_scatter(grad_shift_two, ("dp", "fsdp"), scatter_dimension=0, tiled=True),
        lax.psum_scatter(grad_gain_post, ("dp", "fsdp"), scatter_dimension=0, tiled=True),
        lax.psum_scatter(grad_shift_post, ("dp", "fsdp"), scatter_dimension=0, tiled=True),
        lax.psum_scatter(grad_query, ("dp", "fsdp"), scatter_dimension=0, tiled=True),
    )
    return (
        loss_value.reshape(1),
        grad_tokens,
        grad_text,
        owned[0],
        owned[1],
        owned[2],
        owned[3],
        owned[4],
        owned[5],
        owned[6],
        owned[7],
        owned[8],
        owned[9],
        owned[10],
        owned[11],
        grad_scale,
    )


def solution(mesh):
    in_specs = (
        P(("dp", "fsdp"), None),
        P(("dp", "fsdp"), None),
        P(),
        P(("dp", "fsdp"), None),
        P(),
        P(("dp", "fsdp"), None),
        P(("dp", "fsdp"), None),
        P(("dp", "fsdp"), None),
        P(("dp", "fsdp"), None),
        P(("dp", "fsdp"), None),
        P(("dp", "fsdp")),
        P(("dp", "fsdp")),
        P(("dp", "fsdp")),
        P(("dp", "fsdp")),
        P(("dp", "fsdp")),
        P(("dp", "fsdp")),
        P(("dp", "fsdp")),
    )
    out_specs = (
        P(),
        P(("dp", "fsdp"), None),
        P(("dp", "fsdp"), None),
        P(("dp", "fsdp"), None),
        P(("dp", "fsdp"), None),
        P(("dp", "fsdp"), None),
        P(("dp", "fsdp"), None),
        P(("dp", "fsdp"), None),
        P(("dp", "fsdp")),
        P(("dp", "fsdp")),
        P(("dp", "fsdp")),
        P(("dp", "fsdp")),
        P(("dp", "fsdp")),
        P(("dp", "fsdp")),
        P(("dp", "fsdp")),
        P(),
    )
    return jax.shard_map(shards, mesh=mesh, in_specs=in_specs, out_specs=out_specs, check_vma=False)
```

profile of v0, /device:TPU:1, one launch (start us, length us, event | category | flops | bytes accessed | tf_op | source)
XLA Modules:
  0.0 1484.7 jit_solution(11132809157643250569)
XLA Ops:
  21.8 69.2 %all-reduce.23 = (bf16[768]{0:T(1024)(128)(2,1)S(1)}, bf16[768]{0:T(1024)(128)(2,1)S(1)}, bf16[768]{0:T(1024)(128)(2,1)S(1)}, bf16[768]{0:T(1024)(128)(2,1)S(1)}...) all-reduce(bf16[768]{0:T(1024)(128)(2,1)S(1)} %dynamic-update-slice, ...), channel_id=1, replica_groups=mesh['dp'=8,'fsdp'=16] {'dp','fsdp'}, use_global_device_ids=true, to_apply=%add.1 | all-reduce | flops 5376 | bytes 21504
  94.0 51.6 %all-gather.5 = bf16[128,4,512]{2,1,0:T(4,128)(2,1)S(1)} all-gather(bf16[1,4,512]{2,1,0:T(4,128)(2,1)S(1)} %fusion.56), channel_id=1, replica_groups=mesh['dp'=8,'fsdp'=16] {'dp','fsdp'}, dimensions={0}, use_global_device_ids=true | all-gather | bytes 528384 | tf_op jit(solution)/shard_map/all_gather | solution.py:133
  146.6 62.4 %all-gather.3 = bf16[128,6,512]{2,1,0:T(8,128)(2,1)S(1)} all-gather(bf16[1,6,512]{2,1,0:T(8,128)(2,1)S(1)} %convert_bitcast_fusion.3), channel_id=1, replica_groups=mesh['dp'=8,'fsdp'=16] {'dp','fsdp'}, dimensions={0}, use_global_device_ids=true | all-gather | bytes 792576 | tf_op jit(solution)/shard_map/all_gather | solution.py:72
  227.3 11.8 reshape.275
  281.5 8.1 reshape.268
  289.6 28.0 %multiply_convert_fusion.1 = (bf16[784,3072]{1,0:T(8,128)(2,1)}, f32[784,3072]{1,0:T(8,128)}, f32[784,3072]{1,0:T(8,128)}) fusion(bf16[768,3072]{1,0:T(8,128)(2,1)} %reshape.268, f32[784,768]{1,0:T(8,128)S(1)} %get-tuple-element.72, f32[768]{0:T(1024)S(1)} %convert_element_type.137, f32[768]{0:T(1024)S(1)} %convert_element_type.135, f32[784]{0:T(1024)S(1)} %fusion.58, ...), kind=kOutput, calls=%fused_computation.8 | convolution fusion | flops 3858935808 | bytes 31223936 | tf_op jit(solution)/shard_map/dot_general | solution.py:120
  317.7 8.5 fusion.85
  334.7 55.7 %all-gather.4 = bf16[128,4,512]{2,1,0:T(4,128)(2,1)} all-gather(bf16[1,4,512]{2,1,0:T(4,128)(2,1)S(1)} %fusion.55), channel_id=1, replica_groups=mesh['dp'=8,'fsdp'=16] {'dp','fsdp'}, dimensions={0}, use_global_device_ids=true | all-gather | bytes 528384 | tf_op jit(solution)/shard_map/all_gather | solution.py:132
  413.4 10.1 fusion.70
  423.4 13.3 add_convert_fusion
  436.8 9.1 multiply_reduce_fusion.4
  462.5 12.0 multiply_reduce_fusion
  474.5 12.1 multiply_convert_fusion
  507.2 9.6 convert_element_type.158
  530.8 8.2 fusion.76
  539.0 374.1 %fusion.79 = (f32[8,2304]{1,0:T(8,128)S(1)}, f32[8,768]{1,0:T(8,128)S(1)}, f32[8,3072]{1,0:T(8,128)S(1)}, f32[8,512]{1,0:T(8,128)S(1)}) fusion(f32[768,2304]{1,0:T(8,128)} %fusion.72, f32[768,768]{1,0:T(8,128)} %fusion.47, f32[768,3072]{1,0:T(8,128)} %fusion.76, f32[768,512]{1,0:T(8,128)} %fusion.86), kind=kCustom, calls=%all-reduce-scatter.4 | all-reduce-scatter fusion | flops 6815745 | bytes 20660224
  919.6 12.5 collective-permute-start.122
  932.1 31.2 %collective-permute-start.121 = (f32[8,512]{1,0:T(8,128)S(1)}, f32[8,512]{1,0:T(8,128)S(1)}, u32[]{:S(2)}, u32[]{:S(2)}) collective-permute-start(f32[8,512]{1,0:T(8,128)S(1)} %get-tuple-element.53), channel_id=1, source_target_pairs={{0,26},{1,27},{2,28},{3,29},{4,30},{5,31},{6,32},{7,33},{8,34},{9,... | collective-permute-start | bytes 49160
  1124.0 7.7 collective-permute-start.26
  1214.7 12.6 collective-permute-start.90
  1253.0 65.0 %all-reduce.22 = (f32[768]{0:T(1024)S(1)}, f32[768]{0:T(1024)S(1)}, f32[768]{0:T(1024)S(1)}, f32[768]{0:T(1024)S(1)}, f32[768]{0:T(1024)S(1)}, /*index=5*/f32[768]{0:T(1024)S(1)}, f32[768]{0:T(1024)S(1)}) all-reduce(f32[768]{0:T(1024)} %get-tuple-element.20, ...), channel_id=7, replica_groups=mesh['dp'=8,'fsdp'=16] {'dp','fsdp'}, use_global_device_ids=true, to_apply=%region_38.39.clone | all-reduce | flops 5376 | bytes 43008
  1350.1 16.8 %concatenate.1 = f32[262,768]{1,0:T(8,128)S(1)} concatenate(f32[6,768]{1,0:T(8,128)S(1)} %collective-permute-done.63, f32[8,768]{1,0:T(8,128)S(1)} %collective-permute-done.62, f32[8,768]{1,0:T(8,128)S(1)} %copy-done.101, f32[8,768]{1,0:T(8,128)S(1)} %copy-done.103, f32[8,768]{1,0:T(8,128)S(1)} %copy-done.105, f32[8,768]{1,0:T(8,128)S(1)} %copy-done.107, ...), dimensions={0} | concatenate | bytes 1609728
  1387.7 32.8 %concatenate = f32[262,2304]{1,0:T(8,128)S(1)} concatenate(f32[6,2304]{1,0:T(8,128)} %copy-done.61, f32[8,2304]{1,0:T(8,128)} %copy-done.58, f32[8,2304]{1,0:T(8,128)} %copy-done.59, f32[8,2304]{1,0:T(8,128)} %copy-done.60, f32[8,2304]{1,0:T(8,128)} %copy-done.62, f32[8,2304]{1,0:T(8,128)} %copy-done.63, f32[8,2304]{1,0:T(8,128)} %copy-done.64, f32[8,2304]{1,0:T(8,128)} %copy-done.65, ...), dimensions={0} | concatenate | bytes 4829184
  1443.6 31.5 %concatenate.2 = f32[262,3072]{1,0:T(8,128)S(1)} concatenate(f32[6,3072]{1,0:T(8,128)S(1)} %collective-permute-done.95, f32[8,3072]{1,0:T(8,128)S(1)} %collective-permute-done.94, f32[8,3072]{1,0:T(8,128)} %copy-done.29, f32[8,3072]{1,0:T(8,128)} %copy-done.30, f32[8,3072]{1,0:T(8,128)} %copy-done.31, f32[8,3072]{1,0:T(8,128)} %copy-done.32, f32[8,3072]{1,0:T(8,128)} %copy-done.33, ...), dimensions={0} | concatenate | bytes 6438912
  (827 shorter events, 506.1 us)
Async XLA Ops:
  7.2 202.9 %all-gather.15.cloned.1.call-start = ((), (), s32[]{:S(2)}) async-start(), calls=%async_computation.4 | async-start | bytes 1585152 | tf_op jit(solution)/shard_map/all_gather | solution.py:69
  8.7 205.0 %all-gather.13.cloned.1.call-start = ((), (), s32[]{:S(2)}) async-start(), calls=%async_computation.3 | async-start | bytes 4755456 | tf_op jit(solution)/shard_map/all_gather | solution.py:68
  10.3 271.2 %all-gather.17.cloned.1.call-start = ((), (), s32[]{:S(2)}) async-start(), calls=%async_computation.5 | async-start | bytes 6340608 | tf_op jit(solution)/shard_map/all_gather | solution.py:70
  11.9 305.8 %all-gather.11.cloned.1.call-start = ((), (), s32[]{:S(2)}) async-start(), calls=%async_computation.1 | async-start | bytes 4755456 | tf_op jit(solution)/shard_map/all_gather | solution.py:71
  13.5 1462.3 %reduce-scatter.10.cloned.1.call-start = ((), (), s32[]{:S(2)}) async-start(), calls=%async_computation.2 | async-start | bytes 9510912 | tf_op jit(solution)/shard_map/reduce_scatter | solution.py:206
  914.4 48.9 %collective-permute-start.125 = (f32[8,512]{1,0:T(8,128)S(1)}, f32[8,512]{1,0:T(8,128)S(1)}, u32[]{:S(2)}, u32[]{:S(2)}) collective-permute-start(f32[8,512]{1,0:T(8,128)S(1)} %get-tuple-element.53), channel_id=1, source_target_pairs={{0,30},{1,31},{2,32},{3,33},{4,34},{5,35},{6,36},{7,37},{8,38},{9,... | collective-permute-start | bytes 49160
  917.0 49.5 %collective-permute-start.124 = (f32[8,512]{1,0:T(8,128)S(1)}, f32[8,512]{1,0:T(8,128)S(1)}, u32[]{:S(2)}, u32[]{:S(2)}) collective-permute-start(f32[8,512]{1,0:T(8,128)S(1)} %get-tuple-element.53), channel_id=1, source_target_pairs={{0,29},{1,30},{2,31},{3,32},{4,33},{5,34},{6,35},{7,36},{8,37},{9,... | collective-permute-start | bytes 49160
  918.3 50.7 %collective-permute-start.123 = (f32[8,512]{1,0:T(8,128)S(1)}, f32[8,512]{1,0:T(8,128)S(1)}, u32[]{:S(2)}, u32[]{:S(2)}) collective-permute-start(f32[8,512]{1,0:T(8,128)S(1)} %get-tuple-element.53), channel_id=1, source_target_pairs={{0,28},{1,29},{2,30},{3,31},{4,32},{5,33},{6,34},{7,35},{8,36},{9,... | collective-permute-start | bytes 49160
  919.6 50.7 %collective-permute-start.122 = (f32[8,512]{1,0:T(8,128)S(1)}, f32[8,512]{1,0:T(8,128)S(1)}, u32[]{:S(2)}, u32[]{:S(2)}) collective-permute-start(f32[8,512]{1,0:T(8,128)S(1)} %get-tuple-element.53), channel_id=1, source_target_pairs={{0,27},{1,28},{2,29},{3,30},{4,31},{5,32},{6,33},{7,34},{8,35},{9,... | collective-permute-start | bytes 49160
  932.1 39.6 %collective-permute-start.121 = (f32[8,512]{1,0:T(8,128)S(1)}, f32[8,512]{1,0:T(8,128)S(1)}, u32[]{:S(2)}, u32[]{:S(2)}) collective-permute-start(f32[8,512]{1,0:T(8,128)S(1)} %get-tuple-element.53), channel_id=1, source_target_pairs={{0,26},{1,27},{2,28},{3,29},{4,30},{5,31},{6,32},{7,33},{8,34},{9,... | collective-permute-start | bytes 49160
  1239.6 92.1 %collective-permute-start.83 = (f32[8,3072]{1,0:T(8,128)S(1)}, f32[8,3072]{1,0:T(8,128)S(1)}, u32[]{:S(2)}, u32[]{:S(2)}) collective-permute-start(f32[8,3072]{1,0:T(8,128)S(1)} %get-tuple-element.52), channel_id=1, source_target_pairs={{0,20},{1,21},{2,22},{3,23},{4,24},{5,25},{6,26},{7,27},{8,28},{9,... | collective-permute-start | bytes 294920
  1241.4 94.6 %collective-permute-start.82 = (f32[8,3072]{1,0:T(8,128)S(1)}, f32[8,3072]{1,0:T(8,128)S(1)}, u32[]{:S(2)}, u32[]{:S(2)}) collective-permute-start(f32[8,3072]{1,0:T(8,128)S(1)} %get-tuple-element.52), channel_id=1, source_target_pairs={{0,19},{1,20},{2,21},{3,22},{4,23},{5,24},{6,25},{7,26},{8,27},{9,... | collective-permute-start | bytes 294920
  1243.4 95.3 %collective-permute-start.81 = (f32[8,3072]{1,0:T(8,128)S(1)}, f32[8,3072]{1,0:T(8,128)S(1)}, u32[]{:S(2)}, u32[]{:S(2)}) collective-permute-start(f32[8,3072]{1,0:T(8,128)S(1)} %get-tuple-element.52), channel_id=1, source_target_pairs={{0,18},{1,19},{2,20},{3,21},{4,22},{5,23},{6,24},{7,25},{8,26},{9,... | collective-permute-start | bytes 294920
  1245.4 95.8 %collective-permute-start.80 = (f32[8,3072]{1,0:T(8,128)S(1)}, f32[8,3072]{1,0:T(8,128)S(1)}, u32[]{:S(2)}, u32[]{:S(2)}) collective-permute-start(f32[8,3072]{1,0:T(8,128)S(1)} %get-tuple-element.52), channel_id=1, source_target_pairs={{0,17},{1,18},{2,19},{3,20},{4,21},{5,22},{6,23},{7,24},{8,25},{9,... | collective-permute-start | bytes 294920
  1248.1 96.5 %collective-permute-start.79 = (f32[8,3072]{1,0:T(8,128)S(1)}, f32[8,3072]{1,0:T(8,128)S(1)}, u32[]{:S(2)}, u32[]{:S(2)}) collective-permute-start(f32[8,3072]{1,0:T(8,128)S(1)} %get-tuple-element.52), channel_id=1, source_target_pairs={{0,16},{1,17},{2,18},{3,19},{4,20},{5,21},{6,22},{7,23},{8,24},{9,... | collective-permute-start | bytes 294920
  1331.7 35.2 %collective-permute-start.78 = (f32[8,3072]{1,0:T(8,128)S(1)}, f32[8,3072]{1,0:T(8,128)S(1)}, u32[]{:S(2)}, u32[]{:S(2)}) collective-permute-start(f32[8,3072]{1,0:T(8,128)S(1)} %get-tuple-element.52), channel_id=1, source_target_pairs={{0,15},{1,16},{2,17},{3,18},{4,19},{5,20},{6,21},{7,22},{8,23},{9,... | collective-permute-start | bytes 294920
  1338.7 36.9 %collective-permute-start.76 = (f32[8,3072]{1,0:T(8,128)S(1)}, f32[8,3072]{1,0:T(8,128)S(1)}, u32[]{:S(2)}, u32[]{:S(2)}) collective-permute-start(f32[8,3072]{1,0:T(8,128)S(1)} %get-tuple-element.52), channel_id=1, source_target_pairs={{0,13},{1,14},{2,15},{3,16},{4,17},{5,18},{6,19},{7,20},{8,21},{9,... | collective-permute-start | bytes 294920
  1341.2 38.9 %collective-permute-start.75 = (f32[8,3072]{1,0:T(8,128)S(1)}, f32[8,3072]{1,0:T(8,128)S(1)}, u32[]{:S(2)}, u32[]{:S(2)}) collective-permute-start(f32[8,3072]{1,0:T(8,128)S(1)} %get-tuple-element.52), channel_id=1, source_target_pairs={{0,12},{1,13},{2,14},{3,15},{4,16},{5,17},{6,18},{7,19},{8,20},{9,... | collective-permute-start | bytes 294920
  1344.6 38.4 %collective-permute-start.74 = (f32[8,3072]{1,0:T(8,128)S(1)}, f32[8,3072]{1,0:T(8,128)S(1)}, u32[]{:S(2)}, u32[]{:S(2)}) collective-permute-start(f32[8,3072]{1,0:T(8,128)S(1)} %get-tuple-element.52), channel_id=1, source_target_pairs={{0,11},{1,12},{2,13},{3,14},{4,15},{5,16},{6,17},{7,18},{8,19},{9,... | collective-permute-start | bytes 294920
  1366.9 53.6 %collective-permute-start.73 = (f32[8,3072]{1,0:T(8,128)S(1)}, f32[8,3072]{1,0:T(8,128)S(1)}, u32[]{:S(2)}, u32[]{:S(2)}) collective-permute-start(f32[8,3072]{1,0:T(8,128)S(1)} %get-tuple-element.52), channel_id=1, source_target_pairs={{0,10},{1,11},{2,12},{3,13},{4,14},{5,15},{6,16},{7,17},{8,18},{9,... | collective-permute-start | bytes 294920
  1371.0 51.4 %collective-permute-start.72 = (f32[8,3072]{1,0:T(8,128)S(1)}, f32[8,3072]{1,0:T(8,128)S(1)}, u32[]{:S(2)}, u32[]{:S(2)}) collective-permute-start(f32[8,3072]{1,0:T(8,128)S(1)} %get-tuple-element.52), channel_id=1, source_target_pairs={{0,9},{1,10},{2,11},{3,12},{4,13},{5,14},{6,15},{7,16},{8,17},{9,1... | collective-permute-start | bytes 294920
  1375.6 51.0 %collective-permute-start.71 = (f32[8,3072]{1,0:T(8,128)S(1)}, f32[8,3072]{1,0:T(8,128)S(1)}, u32[]{:S(2)}, u32[]{:S(2)}) collective-permute-start(f32[8,3072]{1,0:T(8,128)S(1)} %get-tuple-element.52), channel_id=1, source_target_pairs={{0,8},{1,9},{2,10},{3,11},{4,12},{5,13},{6,14},{7,15},{8,16},{9,17... | collective-permute-start | bytes 294920
  1380.1 51.4 %collective-permute-start.70 = (f32[8,3072]{1,0:T(8,128)S(1)}, f32[8,3072]{1,0:T(8,128)S(1)}, u32[]{:S(2)}, u32[]{:S(2)}) collective-permute-start(f32[8,3072]{1,0:T(8,128)S(1)} %get-tuple-element.52), channel_id=1, source_target_pairs={{0,7},{1,8},{2,9},{3,10},{4,11},{5,12},{6,13},{7,14},{8,15},{9,16}... | collective-permute-start | bytes 294920
  1383.0 50.6 %collective-permute-start.69 = (f32[8,3072]{1,0:T(8,128)S(1)}, f32[8,3072]{1,0:T(8,128)S(1)}, u32[]{:S(2)}, u32[]{:S(2)}) collective-permute-start(f32[8,3072]{1,0:T(8,128)S(1)} %get-tuple-element.52), channel_id=1, source_target_pairs={{0,6},{1,7},{2,8},{3,9},{4,10},{5,11},{6,12},{7,13},{8,14},{9,15},... | collective-permute-start | bytes 294920
  (318 other events, 15434.7 us)
Sparse Core Ops, SparseCore 0:
  11.4 67.8 all-gather.14
  82.7 64.6 all-gather.12
  151.1 67.2 all-gather.16
  221.6 65.0 all-gather.10
  461.8 241.6 reduce-scatter.9
where the time goes:
time: 1500 us; the launch traced here: 1480 us
  blocking collectives  678 us (45%)
  starting transfers between devices  366 us (24%)
  local copies, waits for them, and re-layouts  196 us (13%)
  matrix products  149 us (10%)
  other arithmetic  61.6 us (4%)
  between operations  24.6 us (2%)
    unnamed x3, blocking collectives  508 us
    unnamed x128, starting transfers between devices  366 us
    unnamed x460, local copies, waits for them, and re-layouts  139 us
    all_gather x1, blocking collectives, shards(): lax.all_gather(w_proj.astype(jnp.bfloat16), ('dp', 'fsdp'), axis=0, tiled...  62.4 us
    all_gather x1, blocking collectives, shards(): lax.all_gather(unit_image.astype(jnp.bfloat16), ('dp', 'fsdp'), axis=0, t...  55.7 us
    all_gather x1, blocking collectives, shards(): lax.all_gather(unit_text.astype(jnp.bfloat16), ('dp', 'fsdp'), axis=0, ti...  51.6 us
  transfers between devices with their start and end apart: 133, of which 5 were waited for; matrix products, arithmetic and copies ran while one was open for 46% of the time, Pallas kernels for 0%

commit v1 on v0

--- a/solution.py
+++ b/solution.py
@@ -4,7 +4,538 @@
 import jax
 import jax.numpy as jnp
 from jax import lax
+from jax.experimental import pallas as pl
+from jax.experimental.pallas import tpu as pltpu
 from jax.sharding import PartitionSpec as P
+
+MESH = pl.DeviceIdType.MESH
+BF = jnp.bfloat16
+F32 = jnp.float32
+
+
+class Place:
+    def __init__(self):
+        dp = lax.axis_index("dp")
+        fs = lax.axis_index("fsdp")
+        self.y, self.core = dp // 2, dp % 2
+        self.z, self.x = fs // 4, fs % 4
+        self.dp, self.fs = dp, fs
+
+    def dev(self, **moved):
+        at = dict(x=self.x, y=self.y, z=self.z, core=self.core)
+        at.update(moved)
+        return (at["y"] * 2 + at["core"], at["z"] * 4 + at["x"])
+
+    def hop(self, dim, step):
+        return self.dev(**{dim: (getattr(self, dim) + step + 4) % 4})
+
+    def sibling(self):
+        return self.dev(core=1 - self.core)
+
+
+class Link:
+    def __init__(self, send, recv, local=None):
+        self.send, self.recv, self.n = send, recv, 0
+        self.open = []
+
+    def copy(self, src, dst, dev):
+        k = self.n
+        self.n += 1
+        c = pltpu.make_async_remote_copy(
+            src_ref=src,
+            dst_ref=dst,
+            send_sem=self.send.at[k],
+            recv_sem=self.recv.at[k],
+            device_id=dev,
+            device_id_type=MESH,
+        )
+        c.start()
+        self.open.append(c)
+        return c
+
+    def drain(self):
+        for c in self.open:
+            c.wait_send()
+        self.open = []
+
+
+ORDERS = (("x", "y", "z"), ("y", "z", "x"), ("z", "x", "y"))
+
+
+def enter(me):
+    sem = pltpu.get_barrier_semaphore()
+    peers = []
+    s = (me.z % 2) * 4 + me.x
+    for k in range(1, 8):
+        t = (s + k) % 8
+        peers.append(me.dev(z=(me.z // 2) * 2 + t // 4, x=t % 4))
+    v = me.dp * 2 + me.z // 2
+    for k in range(1, 16):
+        t = (v + k) % 16
+        peers.append((t // 2, ((t % 2) * 2 + me.z % 2) * 4 + me.x))
+    other = jnp.where(me.z % 2 == 0, (me.z + 3) % 4, (me.z + 1) % 4)
+    peers.append(me.dev(z=other))
+    for p in peers:
+        pl.semaphore_signal(sem, inc=1, device_id=p, device_id_type=MESH)
+    pl.semaphore_wait(sem, len(peers))
+
+
+def half(ref, rows, which):
+    if rows is None:
+        return ref.at[pl.ds(2 * which, 2)]
+    cut = rows // 32 * 16 if rows % 32 == 0 else rows // 32 * 32
+    return ref.at[pl.ds(0, cut)] if which == 0 else ref.at[pl.ds(cut, rows - cut)]
+
+
+def gather_steps(me, link, buf, order, rows):
+    mine = buf.at[me.core]
+    at = [getattr(me, d) for d in order]
+    for stage in range(3):
+        i, d = at[stage], order[stage]
+
+        def block(b, stage=stage):
+            if stage == 0:
+                return mine.at[at[2], at[1], b]
+            if stage == 1:
+                return mine.at[at[2], b]
+            return mine.at[b]
+
+        r = rows if stage == 0 else None
+        lo, hi, far = (i + 3) % 4, (i + 1) % 4, (i + 2) % 4
+        right, left = me.hop(d, 1), me.hop(d, -1)
+        cr = link.copy(block(i), block(i), right)
+        cl = link.copy(block(i), block(i), left)
+        sib = []
+        if stage == 2:
+            sib.append(link.copy(block(i), block(i), me.sibling()))
+        yield
+        cr.wait_recv()
+        fr = link.copy(half(block(lo), r, 0), half(block(lo), r, 0), right)
+        if stage == 2:
+            sib.append(link.copy(block(lo), block(lo), me.sibling()))
+        cl.wait_recv()
+        fl = link.copy(half(block(hi), r, 1), half(block(hi), r, 1), left)
+        if stage == 2:
+            sib.append(link.copy(block(hi), block(hi), me.sibling()))
+        yield
+        fr.wait_recv()
+        fl.wait_recv()
+        if stage == 2:
+            sib.append(link.copy(block(far), block(far), me.sibling()))
+    yield
+    for c in sib:
+        c.wait_recv()
+
+
+def add_into(dst, *srcs):
+    total = dst[...].astype(F32)
+    for s in srcs:
+        total = total + s[...].astype(F32)
+    dst[...] = total.astype(dst.dtype)
+
+
+def add_blocks(dst, srcs, lead):
+    if lead == 0:
+        add_into(dst, *srcs)
+        return
+    n = dst.shape[0]
+    if lead == 1:
+        for a in range(n):
+            add_into(dst.at[a], *[s.at[a] for s in srcs])
+        return
+
+    def body(k, _):
+        a, b = k // dst.shape[1], k % dst.shape[1]
+        add_into(dst.at[a, b], *[s.at[a, b] for s in srcs])
+        return 0
+
+    lax.fori_loop(0, n * dst.shape[1], body, 0)
+
+
+def scatter_steps(me, link, buf, rx, order, rows, finish):
+    rx_core, rx3, rx2, rx1 = rx
+    mine, theirs = buf.at[me.core], buf.at[1 - me.core]
+    at = [getattr(me, d) for d in order]
+    i = at[2]
+    lo, hi, far = (i + 3) % 4, (i + 1) % 4, (i + 2) % 4
+    cores = {}
+    for name, b in (("far", far), ("hi", hi), ("lo", lo), ("i", i)):
+        cores[name] = link.copy(theirs.at[b], rx_core.at[b], me.sibling())
+    yield
+    for stage in (2, 1, 0):
+        i, d = at[stage], order[stage]
+        lo, hi, far = (i + 3) % 4, (i + 1) % 4, (i + 2) % 4
+        right, left = me.hop(d, 1), me.hop(d, -1)
+        r = rows if stage == 0 else None
+        lead = stage
+
+        def block(b, stage=stage):
+            if stage == 0:
+                return mine.at[at[2], at[1], b]
+            if stage == 1:
+                return mine.at[at[2], b]
+            return mine.at[b]
+
+        def settle(name, b, stage=stage):
+            if stage == 2:
+                cores[name].wait_recv()
+                add_blocks(mine.at[b], [rx_core.at[b]], 2)
+
+        R = (rx1, rx2, rx3)[stage]
+        settle("far", far)
+        m0 = link.copy(half(block(far), r, 0), half(R.at[0], r, 0), right)
+        m1 = link.copy(half(block(far), r, 1), half(R.at[0], r, 1), left)
+        settle("hi", hi)
+        d1 = link.copy(half(block(hi), r, 1), half(R.at[1], r, 1), right)
+        settle("lo", lo)
+        d2 = link.copy(half(block(lo), r, 0), half(R.at[2], r, 0), left)
+        yield
+        m0.wait_recv()
+        add_blocks(half(block(hi), r, 0), [half(R.at[0], r, 0)], lead)
+        d3 = link.copy(half(block(hi), r, 0), half(R.at[1], r, 0), right)
+        m1.wait_recv()
+        add_blocks(half(block(lo), r, 1), [half(R.at[0], r, 1)], lead)
+        d4 = link.copy(half(block(lo), r, 1), half(R.at[2], r, 1), left)
+        settle("i", i)
+        yield
+        for c in (d1, d2, d3, d4):
+            c.wait_recv()
+        if stage > 0:
+            add_blocks(block(i), [R.at[1], R.at[2]], lead)
+        else:
+            finish(
+                block(i)[...].astype(F32)
+                + R[1].astype(F32)
+                + R[2].astype(F32)
+            )
+
+
+def run_all(gens):
+    live = list(gens)
+    while live:
+        nxt = []
+        for g in live:
+            try:
+                next(g)
+                nxt.append(g)
+            except StopIteration:
+                pass
+        live = nxt
+
+
+def gather_kernel(
+    qkv, out, up, down, proj, vecs,
+    a0, a1, a2, u0, u1, u2, d0, d1, d2, pj, vo,
+    aloc, arx, urx, drx, prx, vrx, p48, p32, vst, stage, send, recv, lsem,
+):
+    me = Place()
+    link = Link(send, recv)
+    s = (me.z % 2) * 4 + me.x
+    aloc[:, 0:2304] = qkv[...]
+    aloc[:, 2304:3072] = out[...]
+    enter(me)
+    got = {"a": [], "u": [], "v": []}
+    for name, src, rx in (("a", aloc, arx), ("u", up, urx)):
+        for k in range(1, 8):
+            t = (s + k) % 8
+            peer = me.dev(z=(me.z // 2) * 2 + t // 4, x=t % 4)
+            cols = pl.ds(pl.multiple_of(384 * t, 128), 384)
+            got[name].append(link.copy(src.at[:, cols], rx.at[s], peer))
+        if name == "a":
+            for k in range(1, 8):
+                t = (s + k) % 8
+                peer = me.dev(z=(me.z // 2) * 2 + t // 4, x=t % 4)
+                got["v"].append(link.copy(vecs, vrx.at[s], peer))
+    odd = me.x % 2
+    other = pl.ds(pl.multiple_of(384 * (1 - odd), 128), 384)
+    cd = link.copy(down.at[:, other], drx.at[odd], me.dev(x=me.x + 1 - 2 * odd))
+    cp = []
+    for k in range(1, 4):
+        t = (me.x + k) % 4
+        cols = pl.ds(pl.multiple_of(128 * t, 128), 128)
+        cp.append(link.copy(proj.at[:, cols], prx.at[me.x], me.dev(x=t)))
+    own = pl.ds(pl.multiple_of(384 * s, 128), 384)
+    arx[s] = aloc[:, own]
+    urx[s] = up[:, own]
+    drx[odd] = down[:, pl.ds(pl.multiple_of(384 * odd, 128), 384)]
+    prx[me.x] = proj[:, pl.ds(pl.multiple_of(128 * me.x, 128), 128)]
+    vrx[s] = vecs[...]
+
+    n_local = [0]
+
+    def put(src, dst):
+        c = pltpu.make_async_copy(src, dst, lsem.at[n_local[0]])
+        n_local[0] += 1
+        c.start()
+        return c
+
+    gens = []
+    bufs = {"a": (a0, a1, a2), "u": (u0, u1, u2), "d": (d0, d1, d2)}
+    places = [[getattr(me, d) for d in o] for o in ORDERS]
+
+    def piece(ref, c):
+        p = places[c]
+        return ref.at[me.core, p[2], p[1], p[0]]
+
+    for n, name in enumerate(("a", "u", "d")):
+        if name == "d":
+            cd.wait_recv()
+            for j in range(2):
+                p48[24 * j : 24 * j + 24, :] = drx[j]
+        else:
+            for c in got[name]:
+                c.wait_recv()
+            rx = arx if name == "a" else urx
+            for j in range(8):
+                p48[6 * j : 6 * j + 6, :] = rx[j]
+        puts = []
+        for c in range(3):
+            stage[n, c] = p48[:, 128 * c : 128 * c + 128].astype(BF)
+            puts.append(put(stage.at[n, c], piece(bufs[name][c], c)))
+        for c in puts:
+            c.wait()
+        for c in range(3):
+            gens.append(gather_steps(me, link, bufs[name][c], ORDERS[c], 48))
+    for c in cp:
+        c.wait_recv()
+    p32[...] = jnp.zeros_like(p32)
+    for j in range(4):
+        p32[8 * j : 8 * j + 6, :] = prx[j]
+    stage[3, 0, 0:32, :] = p32[...].astype(BF)
+    put(stage.at[3, 0, pl.ds(0, 32)], piece(pj, 0)).wait()
+    gens.append(gather_steps(me, link, pj, ORDERS[0], 32))
+
+    for c in got["v"]:
+        c.wait_recv()
+    total = vrx[0]
+    for j in range(1, 8):
+        total = total + pltpu.roll(vrx[j], 6 * j, 1)
+    v = me.dp * 2 + me.z // 2
+    vst[v] = total
+    cv = []
+    for k in range(1, 16):
+        t = (v + k) % 16
+        peer = (t // 2, ((t % 2) * 2 + me.z % 2) * 4 + me.x)
+        cv.append(link.copy(vst.at[v], vst.at[v], peer))
+    run_all(gens)
+    for c in cv:
+        c.wait_recv()
+    vo[...] = vst[...]
+    link.drain()
+
+
+def gathered(w_qkv, w_out, w_up, w_down, w_proj, vecs):
+    any_ = pl.BlockSpec(memory_space=pl.ANY)
+    vm = pl.BlockSpec(memory_space=pltpu.VMEM)
+    big = jax.ShapeDtypeStruct((2, 4, 4, 4, 48, 128), BF)
+    outs = [big] * 9 + [
+        jax.ShapeDtypeStruct((2, 4, 4, 4, 32, 128), BF),
+        jax.ShapeDtypeStruct((16, 8, 128), F32),
+    ]
+    n = 240
+    return pl.pallas_call(
+        gather_kernel,
+        out_shape=outs,
+        in_specs=[vm] * 6,
+        out_specs=[any_] * 10 + [vm],
+        scratch_shapes=[
+            pltpu.VMEM((6, 3072), F32),
+            pltpu.VMEM((8, 6, 384), F32),
+            pltpu.VMEM((8, 6, 384), F32),
+            pltpu.VMEM((2, 24, 384), F32),
+            pltpu.VMEM((4, 6, 128), F32),
+            pltpu.VMEM((8, 8, 128), F32),
+            pltpu.VMEM((48, 384), F32),
+            pltpu.VMEM((32, 128), F32),
+            pltpu.VMEM((16, 8, 128), F32),
+            pltpu.VMEM((4, 3, 48, 128), BF),
+            pltpu.SemaphoreType.DMA((n,)),
+            pltpu.SemaphoreType.DMA((n,)),
+            pltpu.SemaphoreType.DMA((16,)),
+        ],
+        compiler_params=pltpu.CompilerParams(
+            collective_id=0, has_side_effects=True, vmem_limit_bytes=32 << 20
+        ),
+    )(w_qkv, w_out, w_up, w_down, w_proj, vecs)
+
+
+def scatter_kernel(
+    a0, a1, a2, u0, u1, u2, d0, d1, d2, pj, gv,
+    oqkv, oout, oup, odown, oproj, ovec,
+    rc, r3, r2, r1, pc, p3, p2, p1, tot, ptot, orx, ust, drx, pst, prx, vst, vrx, vst2, vrx2, send, recv,
+):
+    me = Place()
+    link = Link(send, recv)
+    s = (me.z % 2) * 4 + me.x
+    v = me.dp * 2 + me.z // 2
+    enter(me)
+    for k in range(16):
+        lane = 48 * k
+        t, off = lane // 128, lane % 128
+        x0 = gv[:, 128 * t : 128 * t + 128]
+        y0 = pltpu.roll(x0, (128 - off) % 128, 1) if off else x0
+        if off > 80:
+            x1 = gv[:, 128 * t + 128 : 128 * t + 256]
+            y1 = pltpu.roll(x1, (128 - off) % 128, 1)
+            lanes = lax.broadcasted_iota(jnp.int32, (8, 128), 1)
+            y0 = jnp.where(lanes < 128 - off, y0, y1)
+        vst[k] = y0
+    cv = []
+    for k in range(1, 16):
+        t = (v + k) % 16
+        peer = (t // 2, ((t % 2) * 2 + me.z % 2) * 4 + me.x)
+        cv.append(link.copy(vst.at[t], vrx.at[v], peer))
+    vrx[v] = vst[v]
+    bufs = {"d": (d0, d1, d2), "u": (u0, u1, u2), "a": (a0, a1, a2)}
+    gens = []
+
+    def keep(n, c):
+        def finish(total):
+            tot[n, :, 128 * c : 128 * c + 128] = total
+
+        return finish
+
+    def keep_p(total):
+        ptot[...] = total
+
+    for n, name in enumerate(("d", "u", "a")):
+        for c in range(3):
+            k = 3 * n + c
+            gens.append(
+                scatter_steps(
+                    me, link, bufs[name][c],
+                    (rc.at[k], r3.at[k], r2.at[k], r1.at[k]),
+                    ORDERS[c], 48, keep(n, c),
+                )
+            )
+    gens.append(scatter_steps(me, link, pj, (pc, p3, p2, p1), ORDERS[0], 32, keep_p))
+    run_all(gens)
+    for c in cv:
+        c.wait_recv()
+    vtot = vrx[0]
+    for k in range(1, 16):
+        vtot = vtot + vrx[k]
+    vst2[...] = vtot
+    got = []
+    for k in range(1, 8):
+        t = (s + k) % 8
+        peer = me.dev(z=(me.z // 2) * 2 + t // 4, x=t % 4)
+        got.append(link.copy(vst2, vrx2.at[s], peer))
+    vrx2[s] = vst2[...]
+    for n in (1, 2):
+        for j in range(8):
+            ust[n - 1, j] = tot[n, 6 * j : 6 * j + 6, :]
+        for k in range(1, 8):
+            t = (s + k) % 8
+            peer = me.dev(z=(me.z // 2) * 2 + t // 4, x=t % 4)
+            got.append(link.copy(ust.at[n - 1, t], orx.at[n - 1, s], peer))
+        orx[n - 1, s] = ust[n - 1, s]
+    odd = me.x % 2
+    got.append(
+        link.copy(
+            tot.at[0, pl.ds(pl.multiple_of(24 * (1 - odd), 8), 24)],
+            drx.at[odd],
+            me.dev(x=me.x + 1 - 2 * odd),
+        )
+    )
+    drx[odd] = tot[0, pl.ds(pl.multiple_of(24 * odd, 8), 24), :]
+    for j in range(4):
+        pst[j] = ptot[8 * j : 8 * j + 6, :]
+    for k in range(1, 4):
+        t = (me.x + k) % 4
+        got.append(link.copy(pst.at[t], prx.at[me.x], me.dev(x=t)))
+    prx[me.x] = pst[me.x]
+    for c in got:
+        c.wait_recv()
+    vtot = vrx2[0]
+    for k in range(1, 8):
+        vtot = vtot + vrx2[k]
+    ovec[...] = pltpu.roll(vtot, (128 - 6 * s) % 128, 1)
+    for j in range(8):
+        oup[:, 384 * j : 384 * j + 384] = orx[0, j]
+        if j < 6:
+            oqkv[:, 384 * j : 384 * j + 384] = orx[1, j]
+        else:
+            oout[:, 384 * (j - 6) : 384 * (j - 6) + 384] = orx[1, j]
+    for j in range(2):
+        odown[:, 384 * j : 384 * j + 384] = drx[j]
+    for j in range(4):
+        oproj[:, 128 * j : 128 * j + 128] = prx[j]
+    link.drain()
+
+
+def scattered(bufs, gv):
+    vm = pl.BlockSpec(memory_space=pltpu.VMEM)
+    n = 340
+    S = jax.ShapeDtypeStruct
+    V = pltpu.VMEM
+    return pl.pallas_call(
+        scatter_kernel,
+        out_shape=[
+            S((6, 2304), F32), S((6, 768), F32), S((6, 3072), F32), S((24, 768), F32), S((6, 512), F32), S((8, 128), F32)
+        ],
+        in_specs=[vm] * 11,
+        out_specs=[vm] * 6,
+        scratch_shapes=[
+            V((9, 4, 4, 4, 48, 128), BF), V((9, 3, 4, 4, 48, 128), BF), V((9, 3, 4, 48, 128), BF), V((9, 3, 48, 128), BF),
+            V((4, 4, 4, 32, 128), BF), V((3, 4, 4, 32, 128), BF), V((3, 4, 32, 128), BF), V((3, 32, 128), BF),
+            V((3, 48, 384), F32), V((32, 128), F32), V((2, 8, 6, 384), F32), V((2, 8, 6, 384), F32),
+            V((2, 24, 384), F32), V((4, 6, 128), F32), V((4, 6, 128), F32),
+            V((16, 8, 128), F32), V((16, 8, 128), F32), V((8, 128), F32), V((8, 8, 128), F32),
+            pltpu.SemaphoreType.DMA((n,)),
+            pltpu.SemaphoreType.DMA((n,)),
+        ],
+        compiler_params=pltpu.CompilerParams(
+            collective_id=1, has_side_effects=True, vmem_limit_bytes=56 << 20
+        ),
+    )(*bufs, gv)
+
+
+def canonical(buf, c):
+    names = ("core",) + ORDERS[c][::-1]
+    return jnp.transpose(buf, [names.index(d) for d in ("y", "core", "z", "x")] + [4, 5])
+
+
+def classed(arr, c):
+    names = ("y", "core", "z", "x")
+    want = ("core",) + ORDERS[c][::-1]
+    return jnp.transpose(arr, [names.index(d) for d in want] + [4, 5])
+
+
+def wide(bufs):
+    full = jnp.stack([canonical(b, c) for c, b in enumerate(bufs)], axis=5)
+    full = full.reshape(4, 2, 2, 2, 4, 48, 3, 128)
+    return jnp.transpose(full, (0, 1, 2, 5, 3, 4, 6, 7)).reshape(768, 3072)
+
+
+def narrow(mat):
+    full = mat.reshape(4, 2, 2, 48, 2, 4, 3, 128)
+    full = jnp.transpose(full, (6, 0, 1, 2, 4, 5, 3, 7)).reshape(3, 4, 2, 4, 4, 48, 128)
+    return [classed(full[c], c) for c in range(3)]
+
+
+def tall(bufs):
+    full = jnp.stack([canonical(b, c) for c, b in enumerate(bufs)], axis=5)
+    full = full.reshape(4, 2, 4, 2, 2, 48, 3, 128)
+    return jnp.transpose(full, (0, 1, 2, 3, 5, 4, 6, 7)).reshape(3072, 768)
+
+
+def untall(mat):
+    full = mat.reshape(4, 2, 4, 2, 48, 2, 3, 128)
+    full = jnp.transpose(full, (6, 0, 1, 2, 3, 5, 4, 7)).reshape(3, 4, 2, 4, 4, 48, 128)
+    return [classed(full[c], c) for c in range(3)]
+
+
+def proj_of(buf):
+    full = canonical(buf, 0)
+    full = jnp.transpose(full, (0, 1, 2, 4, 3, 5)).reshape(128, 8, 512)
+    return full[:, :6].reshape(768, 512)
+
+
+def proj_back(mat):
+    full = jnp.pad(mat.reshape(128, 6, 512), ((0, 0), (0, 2), (0, 0))).reshape(4, 2, 4, 32, 4, 128)
+    return classed(jnp.transpose(full, (0, 1, 2, 4, 3, 5)), 0)
+
 
 HEADS = 12
 HDIM = 64
@@ -64,34 +595,21 @@
     shift_post,
     pool_query,
 ):
-    gathered = (
-        lax.all_gather(w_qkv.astype(jnp.bfloat16), ("dp", "fsdp"), axis=0, tiled=True),
-        lax.all_gather(w_out.astype(jnp.bfloat16), ("dp", "fsdp"), axis=0, tiled=True),
-        lax.all_gather(w_up.astype(jnp.bfloat16), ("dp", "fsdp"), axis=0, tiled=True),
-        lax.all_gather(w_down.astype(jnp.bfloat16), ("dp", "fsdp"), axis=0, tiled=True),
-        lax.all_gather(w_proj.astype(jnp.bfloat16), ("dp", "fsdp"), axis=0, tiled=True),
-        lax.all_gather(gain_one.astype(jnp.bfloat16), ("dp", "fsdp"), axis=0, tiled=True),
-        lax.all_gather(shift_one.astype(jnp.bfloat16), ("dp", "fsdp"), axis=0, tiled=True),
-        lax.all_gather(gain_two.astype(jnp.bfloat16), ("dp", "fsdp"), axis=0, tiled=True),
-        lax.all_gather(shift_two.astype(jnp.bfloat16), ("dp", "fsdp"), axis=0, tiled=True),
-        lax.all_gather(gain_post.astype(jnp.bfloat16), ("dp", "fsdp"), axis=0, tiled=True),
-        lax.all_gather(shift_post.astype(jnp.bfloat16), ("dp", "fsdp"), axis=0, tiled=True),
-        lax.all_gather(pool_query.astype(jnp.bfloat16), ("dp", "fsdp"), axis=0, tiled=True),
-    )
-    qkv_full, out_full, up_full, down_full, proj_full = (
-        gathered[0],
-        gathered[1],
-        gathered[2],
-        gathered[3],
-        gathered[4],
-    )
-    gain_first = gathered[5].astype(jnp.float32)
-    shift_first = gathered[6].astype(jnp.float32)
-    gain_second = gathered[7].astype(jnp.float32)
-    shift_second = gathered[8].astype(jnp.float32)
-    gain_last = gathered[9].astype(jnp.float32)
-    shift_last = gathered[10].astype(jnp.float32)
-    query_full = gathered[11].astype(jnp.float32)
+    vecs = jnp.stack(
+        [gain_one, shift_one, gain_two, shift_two, gain_post, shift_post, pool_query]
+    )
+    vecs = jnp.pad(vecs.astype(BF).astype(F32), ((0, 1), (0, 122)))
+    got = gathered(w_qkv, w_out, w_up, w_down, w_proj, vecs)
+    mat_a = wide(got[0:3])
+    qkv_full, out_full = mat_a[:, :2304], mat_a[:, 2304:]
+    up_full = wide(got[3:6])
+    down_full = tall(got[6:9])
+    proj_full = proj_of(got[9])
+    vec_full = jnp.transpose(got[10][:, :, :48], (1, 0, 2)).reshape(8, 768)
+    gain_first, shift_first, gain_second, shift_second, gain_last, shift_last, query_full = [
+        vec_full[k] for k in range(7)
+    ]
+    qkv_back, out_back, up_back, down_back, proj_back_w = qkv_full, out_full, up_full, down_full, proj_full
     images_here, patches = keep_mask.shape
     model_width = tokens.shape[1]
     row_count = images_here * patches
@@ -144,15 +662,8 @@
     grad_unit_text = lax.dynamic_slice_in_dim(grad_text_all, offset, images_here, 0)
     grad_text = text_back(grad_unit_text)[0]
     grad_embed = unit_back(grad_unit)[0].astype(jnp.bfloat16)
-    qkv_back, out_back, up_back, down_back, proj_back = (
-        lax.all_gather(w_qkv.astype(jnp.bfloat16), ("dp", "fsdp"), axis=0, tiled=True),
-        lax.all_gather(w_out.astype(jnp.bfloat16), ("dp", "fsdp"), axis=0, tiled=True),
-        lax.all_gather(w_up.astype(jnp.bfloat16), ("dp", "fsdp"), axis=0, tiled=True),
-        lax.all_gather(w_down.astype(jnp.bfloat16), ("dp", "fsdp"), axis=0, tiled=True),
-        lax.all_gather(w_proj.astype(jnp.bfloat16), ("dp", "fsdp"), axis=0, tiled=True),
-    )
     grad_proj = jnp.dot(pooled_half.T, grad_embed, preferred_element_type=jnp.float32)
-    grad_pooled = jnp.dot(grad_embed, proj_back.T, preferred_element_type=jnp.float32)
+    grad_pooled = jnp.dot(grad_embed, proj_back_w.T, preferred_element_type=jnp.float32)
     grad_second, grad_gain_post, grad_shift_post, grad_query = pool_back(grad_pooled)
     grad_branch_two = grad_second.astype(jnp.bfloat16)
     grad_down = jnp.dot(active.T, grad_branch_two, preferred_element_type=jnp.float32)
@@ -199,20 +710,16 @@
     grad_normed = jnp.dot(grad_mixed, qkv_back.T, preferred_element_type=jnp.float32)
     grad_input_norm, grad_gain_one, grad_shift_one = norm_one_back(grad_normed)
     grad_tokens = grad_first + grad_input_norm
-    owned = (
-        lax.psum_scatter(grad_qkv, ("dp", "fsdp"), scatter_dimension=0, tiled=True),
-        lax.psum_scatter(grad_out, ("dp", "fsdp"), scatter_dimension=0, tiled=True),
-        lax.psum_scatter(grad_up, ("dp", "fsdp"), scatter_dimension=0, tiled=True),
-        lax.psum_scatter(grad_down, ("dp", "fsdp"), scatter_dimension=0, tiled=True),
-        lax.psum_scatter(grad_proj, ("dp", "fsdp"), scatter_dimension=0, tiled=True),
-        lax.psum_scatter(grad_gain_one, ("dp", "fsdp"), scatter_dimension=0, tiled=True),
-        lax.psum_scatter(grad_shift_one, ("dp", "fsdp"), scatter_dimension=0, tiled=True),
-        lax.psum_scatter(grad_gain_two, ("dp", "fsdp"), scatter_dimension=0, tiled=True),
-        lax.psum_scatter(grad_shift_two, ("dp", "fsdp"), scatter_dimension=0, tiled=True),
-        lax.psum_scatter(grad_gain_post, ("dp", "fsdp"), scatter_dimension=0, tiled=True),
-        lax.psum_scatter(grad_shift_post, ("dp", "fsdp"), scatter_dimension=0, tiled=True),
-        lax.psum_scatter(grad_query, ("dp", "fsdp"), scatter_dimension=0, tiled=True),
-    )
+    grads_a = narrow(jnp.concatenate([grad_qkv, grad_out], axis=1).astype(BF))
+    grads_u = narrow(grad_up.astype(BF))
+    grads_d = untall(grad_down.astype(BF))
+    grads_p = proj_back(grad_proj.astype(BF))
+    grads_v = jnp.stack(
+        [grad_gain_one, grad_shift_one, grad_gain_two, grad_shift_two, grad_gain_post, grad_shift_post, grad_query]
+    )
+    grads_v = jnp.pad(grads_v, ((0, 1), (0, 0)))
+    *mats, vec_out = scattered((*grads_a, *grads_u, *grads_d, grads_p), grads_v)
+    owned = (*mats, *[vec_out[k, :6] for k in range(7)])
     return (
         loss_value.reshape(1),
         grad_tokens,

time: 1500 us -> 723 us (0.48)
  blocking collectives: 678 us -> 110 us
  starting transfers between devices: 366 us -> 0 us
  Pallas kernels: 0 us -> 111 us
  local copies, waits for them, and re-layouts: 196 us -> 269 us
  other arithmetic: 61.6 us -> 87.7 us
  matrix products: 149 us -> 129 us
  between operations: 24.6 us -> 7.78 us
    unnamed x3 -> x0, blocking collectives: 508 us -> none
    unnamed x128 -> x0, starting transfers between devices: 366 us -> none
    pallas_call x0 -> x2, Pallas kernels: none -> 111 us  [the longest x1 58.4 us: scattered(): pl.pallas_call(scatter_kernel, out_shape=[S((6, 2304), F32), S((6, 768),...]
    unnamed x460 -> x166, local copies, waits for them, and re-layouts: 139 us -> 39.9 us
    reshape x0 -> x16, local copies, waits for them, and re-layouts: none -> 70.6 us  [the longest x2 24.9 us: wide(): return jnp.transpose(full, (0, 1, 2, 5, 3, 4, 6, 7)).reshape(768, 3072)]
    all_gather x1 -> x0, blocking collectives: 62.4 us -> none  [shards(): lax.all_gather(w_proj.astype(jnp.bfloat16), ('dp', 'fsdp'), axis=0, tiled...]
    slice x0 -> x13, local copies, waits for them, and re-layouts: none -> 49 us  [the longest x8 33.5 us: narrow(): return [classed(full[c], c) for c in range(3)]]
    another operation x0 -> x13, local copies, waits for them, and re-layouts: none -> 36.1 us  [the longest x6 21.7 us: wide(): full = jnp.stack([canonical(b, c) for c, b in enumerate(bufs)], axis=5)]
  transfers between devices with their start and end apart: 133 -> 0, of which waited for: 5 -> 0; matrix products, arithmetic and copies ran while one was open for 46% -> 0% of each run, Pallas kernels for 0% -> 0%
where the time goes in v1:
time: 723 us; the launch traced here: 715 us
  local copies, waits for them, and re-layouts  269 us (37%)
  matrix products  129 us (18%)
  Pallas kernels  111 us (15%)
  blocking collectives  110 us (15%)
  other arithmetic  87.7 us (12%)
  between operations  7.78 us (1%)
    pallas_call x1, Pallas kernels, scattered(): pl.pallas_call(scatter_kernel, out_shape=[S((6, 2304), F32), S((6, 768),...  58.4 us
    all_gather x1, blocking collectives, shards(): lax.all_gather(unit_text.astype(jnp.bfloat16), ('dp', 'fsdp'), axis=0, ti...  55.7 us
    all_gather x1, blocking collectives, shards(): lax.all_gather(unit_image.astype(jnp.bfloat16), ('dp', 'fsdp'), axis=0, t...  53.8 us
    pallas_call x1, Pallas kernels, gathered(): pl.pallas_call(gather_kernel, out_shape=outs, in_specs=[vm] * 6, out_spec...  52.4 us
    unnamed x166, local copies, waits for them, and re-layouts  39.9 us
    slice x8, local copies, waits for them, and re-layouts, narrow(): return [classed(full[c], c) for c in range(3)]  33.5 us
    dot_general x1, matrix products, shards(): upward = jnp.dot(normed_two, up_full, preferred_element_type=jnp.float32)  28 us
    reshape x2, local copies, waits for them, and re-layouts, wide(): return jnp.transpose(full, (0, 1, 2, 5, 3, 4, 6, 7)).reshape(768, 3072)  24.9 us

profile of v1, /device:TPU:1, one launch (start us, length us, event | category | flops | bytes accessed | tf_op | source)
XLA Modules:
  0.0 714.5 jit_solution(1483722374060186373)
XLA Ops:
  10.4 55.7 %all-gather.1 = bf16[128,4,512]{2,1,0:T(4,128)(2,1)S(1)} all-gather(bf16[1,4,512]{2,1,0:T(4,128)(2,1)S(1)} %fusion.56), channel_id=1, replica_groups=mesh['dp'=8,'fsdp'=16] {'dp','fsdp'}, dimensions={0}, use_global_device_ids=true | all-gather | bytes 528384 | tf_op jit(solution)/shard_map/all_gather | solution.py:651
  67.1 52.4 %shard_map.288 = (bf16[2,4,4,4,48,128]{5,4,3,2,1,0:T(8,128)(2,1)S(1)}, bf16[2,4,4,4,48,128]{5,4,3,2,1,0:T(8,128)(2,1)S(1)}, bf16[2,4,4,4,48,128]{5,4,3,2,1,0:T(8...) custom-call(f32[6,2304]{1,0:T(8,128)S(1)} %copy-done.13, ...), custom_call_target="tpu_custom_call" | custom-call | tf_op jit(solution)/shard_map/pallas_call | solution.py:336
  149.3 12.1 %maximum_bitcast_fusion = bf16[4,2,2,48,2,4,3,128]{7,6,5,4,3,2,1,0:T(4,128)(2,1)} fusion(bf16[4,2,2,2,4,48,1,128]{7,6,4,3,5,2,1,0:T(2,128)(2,1)S(1)} %copy.94, bf16[4,2,2,2,4,48,1,128]{7,6,4,3,5,2,1,0:T(2,128)(2,1)S(1)} %copy.93, bf16[4,2,2,2,4,48,1,128]{7,6,4,3,5,2,1,0:T(2,128)(2,1)S(1)} %copy.92), kind=kLoop, calls=%fused_computation.23 | loop fusion | flops 14155776 | bytes 9437184 | tf_op jit(solution)/shard_map/transpose | solution.py:508
  161.4 12.4 %reshape.339 = bf16[768,3072]{1,0:T(8,128)(2,1)} reshape(bf16[4,2,2,48,2,4,3,128]{7,6,5,4,3,2,1,0:T(4,128)(2,1)} %maximum_bitcast_fusion) | data formatting | bytes 9437184 | tf_op jit(solution)/shard_map/reshape | solution.py:508
  184.6 11.6 %maximum_bitcast_fusion.1 = bf16[4,2,2,48,2,4,3,128]{7,6,5,4,3,2,1,0:T(4,128)(2,1)} fusion(bf16[4,2,2,2,4,48,1,128]{7,6,4,3,5,2,1,0:T(2,128)(2,1)S(1)} %copy.103, bf16[4,2,2,2,4,48,1,128]{7,6,4,3,5,2,1,0:T(2,128)(2,1)S(1)} %copy.102, bf16[4,2,2,2,4,48,1,128]{7,6,4,3,5,2,1,0:T(2,128)(2,1)S(1)} %copy.101), kind=kLoop, calls=%fused_computation.24 | loop fusion | flops 14155776 | bytes 9437184 | tf_op jit(solution)/shard_map/transpose | solution.py:508
  196.2 12.5 %reshape.342 = bf16[768,3072]{1,0:T(8,128)(2,1)} reshape(bf16[4,2,2,48,2,4,3,128]{7,6,5,4,3,2,1,0:T(4,128)(2,1)} %maximum_bitcast_fusion.1) | data formatting | bytes 9437184 | tf_op jit(solution)/shard_map/reshape | solution.py:508
  220.4 11.6 %maximum_bitcast_fusion.2 = bf16[4,2,4,2,48,2,3,128]{7,6,5,4,3,2,1,0:T(4,128)(2,1)} fusion(bf16[4,2,4,2,2,48,1,128]{7,6,4,5,3,2,1,0:T(2,128)(2,1)S(1)} %copy.106, bf16[4,2,4,2,2,48,1,128]{7,6,4,5,3,2,1,0:T(2,128)(2,1)S(1)} %copy.105, bf16[4,2,4,2,2,48,1,128]{7,6,4,5,3,2,1,0:T(2,128)(2,1)S(1)} %copy.104), kind=kLoop, calls=%fused_computation.25 | loop fusion | flops 14155776 | bytes 9437184 | tf_op jit(solution)/shard_map/transpose | solution.py:520
  232.0 12.5 %reshape.343 = bf16[3072,768]{1,0:T(8,128)(2,1)} reshape(bf16[4,2,4,2,48,2,3,128]{7,6,5,4,3,2,1,0:T(4,128)(2,1)} %maximum_bitcast_fusion.2) | data formatting | bytes 9437184 | tf_op jit(solution)/shard_map/reshape | solution.py:520
  251.4 12.0 %reshape.363 = bf16[4,196,3,12,64]{4,3,2,1,0:T(8,128)(2,1)} reshape(bf16[784,2304]{1,0:T(8,128)(2,1)} %convolution_convert_fusion) | data formatting | bytes 7225344 | tf_op jit(solution)/shard_map/reshape | solution.py:622
  302.7 28.0 %multiply_convert_fusion.1 = (bf16[784,3072]{1,0:T(8,128)(2,1)S(1)}, f32[784,3072]{1,0:T(8,128)}, f32[784,3072]{1,0:T(8,128)}) fusion(bf16[768,3072]{1,0:T(8,128)(2,1)} %reshape.342, f32[784,768]{1,0:T(8,128)S(1)} %get-tuple-element.107, f32[768]{0:T(1024)S(1)} %add.129, f32[768]{0:T(1024)S(1)} %mul.409, f32[784]{0:T(1024)S(1)} %fusion.58, ...), kind=kOutput, calls=%fused_computation.8 | convolution fusion | flops 3858935808 | bytes 31223936 | tf_op jit(solution)/shard_map/dot_general | solution.py:638
  343.4 53.8 %all-gather = bf16[128,4,512]{2,1,0:T(4,128)(2,1)} all-gather(bf16[1,4,512]{2,1,0:T(4,128)(2,1)S(1)} %fusion.55), channel_id=1, replica_groups=mesh['dp'=8,'fsdp'=16] {'dp','fsdp'}, dimensions={0}, use_global_device_ids=true | all-gather | bytes 528384 | tf_op jit(solution)/shard_map/all_gather | solution.py:650
  434.3 12.8 %add_convert_fusion = bf16[784,3072]{1,0:T(8,128)(2,1)} fusion(f32[784,3072]{1,0:T(8,128)} %get-tuple-element.80, f32[784,3072]{1,0:T(8,128)} %get-tuple-element.108, bf16[3072,768]{1,0:T(8,128)(2,1)} %reshape.343, f32[784,768]{1,0:T(8,128)S(1)} %get-tuple-element.76, f32[784]{0:T(1024)S(1)} %negate_multiply_fusion.3), kind=kOutput, calls=%fused_computation.7 | convolution fusion | flops 3734298624 | bytes 31214656 | tf_op jit(solution)/shard_map/dot_general | solution.py:670
  454.0 8.2 %convolution_convert_fusion.2 = bf16[768,3072]{1,0:T(8,128)(2,1)} fusion(bf16[784,3072]{1,0:T(8,128)(2,1)S(1)} %copy-done.65, f32[784,768]{1,0:T(8,128)S(1)} %copy-done.26, f32[768]{0:T(1024)S(1)} %add.129, f32[768]{0:T(1024)S(1)} %mul.409, f32[784]{0:T(1024)S(1)} %fusion.58, f32[784]{0:T(1024)S(1)} %broadcast_multiply_fusion.2), kind=kOutput, calls=%fused_computation.29 | convolution fusion | flops 3704745984 | bytes 11956352 | tf_op jit(solution)/shard_map/dot_general | solution.py:672
  462.2 9.7 %convolution_convert_fusion.1 = bf16[3072,768]{1,0:T(8,128)(2,1)} fusion(bf16[784,3072]{1,0:T(8,128)(2,1)} %copy-done.66, f32[784,768]{1,0:T(8,128)S(1)} %get-tuple-element.76, f32[784]{0:T(1024)S(1)} %negate_multiply_fusion.3), kind=kOutput, calls=%fused_computation.28 | convolution fusion | flops 3702939648 | bytes 11947072 | tf_op jit(solution)/shard_map/dot_general | solution.py:669
  478.1 11.3 %reshape.350 = bf16[4,2,4,2,48,2,3,128]{7,6,5,4,3,2,1,0:T(4,128)(2,1)} reshape(bf16[3072,768]{1,0:T(8,128)(2,1)} %convolution_convert_fusion.1) | data formatting | bytes 9437184 | tf_op jit(solution)/shard_map/reshape | solution.py:524
  489.4 13.6 %reshape.349 = bf16[4,2,2,48,2,4,3,128]{7,6,5,4,3,2,1,0:T(4,128)(2,1)} reshape(bf16[768,3072]{1,0:T(8,128)(2,1)} %convolution_convert_fusion.2) | data formatting | bytes 9437184 | tf_op jit(solution)/shard_map/reshape | solution.py:512
  511.2 7.8 %fusion.33 = bf16[4,196,1,12,64]{1,4,3,0,2:T(8,128)(2,1)} fusion(bf16[4,196,12,64]{1,3,2,0:T(8,128)(2,1)} %copy.109, f32[4,12,196,196]{2,3,1,0:T(8,128)} %copy-done.17, f32[4,12,196]{2,1,0:T(8,128)S(1)} %copy-done.39, pred[4,196]{1,0:T(4,128)(4,1)S(1)} %copy-done.56), kind=kOutput, calls=%fused_computation.86 | convolution fusion | flops 244005888 | bytes 9822736 | tf_op jit(solution)/shard_map/bhqk,bqhd->bkhd/dot_general | solution.py:689
  519.0 9.7 %fusion.80 = (bf16[1,4,2,2,2,4,48,128]{7,0,5,4,6,3,2,1:T(2,128)(2,1)S(1)}, bf16[1,4,2,2,2,4,48,128]{7,0,5,4,6,3,2,1:T(2,128)(2,1)S(1)}, bf16[1,4,2,2,2,4,48,128]{7,0,5,4,6,3,2,1:T(2,128)(2,1)S(1)}) fusion(bf16[3,4,2,2,2,4,48,128]{7,0,5,4,6,3,2,1:T(4,128)(2,1)S(1)} %bitcast.191), kind=kLoop, calls=%fused_computation.197 | loop fusion | bytes 9437184 | tf_op jit(solution)/shard_map/slice | solution.py:514
  534.1 10.6 %fusion.79 = (bf16[1,4,2,4,2,2,48,128]{7,0,5,6,4,3,2,1:T(2,128)(2,1)S(1)}, bf16[1,4,2,4,2,2,48,128]{7,0,5,6,4,3,2,1:T(2,128)(2,1)S(1)}, bf16[1,4,2,4,2,2,48,128]{7,0,5,6,4,3,2,1:T(2,128)(2,1)S(1)}) fusion(bf16[3,4,2,4,2,2,48,128]{7,0,5,6,4,3,2,1:T(4,128)(2,1)S(1)} %bitcast.188), kind=kLoop, calls=%fused_computation.196 | loop fusion | bytes 9437184 | tf_op jit(solution)/shard_map/slice | solution.py:526
  556.4 11.9 %multiply_convert_fusion = bf16[4,12,196,196]{2,3,1,0:T(8,128)(2,1)} fusion(f32[4,12,196,196]{2,3,1,0:T(8,128)} %get-tuple-element.116, f32[4,12,196,196]{2,3,1,0:T(8,128)} %copy-done.17, f32[4,12,196]{2,1,0:T(8,128)S(1)} %get-tuple-element.115, f32[4,12,196]{2,1,0:T(8,128)S(1)} %copy-done.39, pred[4,196]{1,0:T(4,128)(4,1)S(1)} %copy-done.56), kind=kLoop, calls=%fused_computation.1 | loop fusion | flops 11063808 | bytes 18515728 | tf_op jit(solution)/shard_map/convert_element_type | solution.py:698
  582.1 9.7 %convert_element_type.99 = bf16[784,2304]{0,1:T(8,128)(2,1)} reshape(bf16[4,196,3,12,64]{1,0,4,3,2:T(4,128)(2,1)} %copy.114) | data formatting | bytes 7225344 | tf_op jit(solution)/shard_map/convert_element_type | solution.py:707
  612.7 13.6 %convert_element_type.100 = bf16[4,2,2,48,2,4,3,128]{7,6,5,4,3,2,1,0:T(4,128)(2,1)} reshape(bf16[768,3072]{1,0:T(8,128)(2,1)} %pad_maximum_fusion.1) | data formatting | bytes 9437184 | tf_op jit(solution)/shard_map/convert_element_type | solution.py:713
  626.3 13.2 %fusion.81 = (bf16[1,4,2,2,2,4,48,128]{7,0,5,4,6,3,2,1:T(2,128)(2,1)S(1)}, bf16[1,4,2,2,2,4,48,128]{7,0,5,4,6,3,2,1:T(2,128)(2,1)S(1)}, bf16[1,4,2,2,2,4,48,128]{7,0,5,4,6,3,2,1:T(2,128)(2,1)S(1)}) fusion(bf16[3,4,2,2,2,4,48,128]{7,0,5,4,6,3,2,1:T(4,128)(2,1)} %bitcast.192), kind=kLoop, calls=%fused_computation.198 | loop fusion | bytes 9437184 | tf_op jit(solution)/shard_map/slice | solution.py:514
  644.7 58.4 %shard_map.289 = (f32[6,2304]{1,0:T(8,128)}, f32[6,768]{1,0:T(8,128)}, f32[6,3072]{1,0:T(8,128)}, f32[24,768]{1,0:T(8,128)}, f32[6,512]{1,0:T(8,128)}, /*index=5*/f32[8,128]{1,0:T(8,128)}) custom-call(bf16[2,4,4,4,48,128]{5,4,3,2,1,0:T(8,128)(2,1)} %bitcast.201, bf16[2,4,4,4,48,128]{5,4,3,2,1,0:T(8,128)(2,1)} %bitcast.200, ...), custom_call_target="tpu_custom_call" | custom-call | tf_op jit(solution)/shard_map/pallas_call | solution.py:472
  (309 shorter events, 241.7 us)
Async XLA Ops:
  0.6 66.5 %copy-start.16 = (f32[6,512]{1,0:T(8,128)S(1)}, f32[6,512]{1,0:T(8,128)}, u32[]{:S(2)}) copy-start(f32[6,512]{1,0:T(8,128)} %proj.1) | copy-start | bytes 36868
  0.7 66.5 %copy-start.14 = (f32[24,768]{1,0:T(8,128)S(1)}, f32[24,768]{1,0:T(8,128)}, u32[]{:S(2)}) copy-start(f32[24,768]{1,0:T(8,128)} %down.1) | copy-start | bytes 221188
  0.7 66.5 %copy-start.12 = (f32[6,3072]{1,0:T(8,128)S(1)}, f32[6,3072]{1,0:T(8,128)}, u32[]{:S(2)}) copy-start(f32[6,3072]{1,0:T(8,128)} %up.1) | copy-start | bytes 221188
  0.7 66.4 %copy-start.15 = (f32[6,768]{1,0:T(8,128)S(1)}, f32[6,768]{1,0:T(8,128)}, u32[]{:S(2)}) copy-start(f32[6,768]{1,0:T(8,128)} %out.1) | copy-start | bytes 55300
  0.7 66.4 %copy-start.13 = (f32[6,2304]{1,0:T(8,128)S(1)}, f32[6,2304]{1,0:T(8,128)}, u32[]{:S(2)}) copy-start(f32[6,2304]{1,0:T(8,128)} %qkv.1) | copy-start | bytes 165892
  3.7 287.2 %copy-start.55 = (pred[4,196]{1,0:T(4,128)(4,1)}, pred[4,196]{1,0:T(4,128)(4,1)S(1)}, u32[]{:S(2)}) copy-start(pred[4,196]{1,0:T(4,128)(4,1)S(1)} %broadcast_compare_fusion) | copy-start | bytes 2356
  8.0 236.5 %copy-start.45 = (f32[784]{0:T(1024)}, f32[784]{0:T(1024)S(1)}, u32[]{:S(2)}) copy-start(f32[784]{0:T(1024)S(1)} %broadcast_multiply_fusion.3) | copy-start | bytes 9412
  10.4 234.1 %copy-start.49 = (f32[784]{0:T(1024)}, f32[784]{0:T(1024)S(1)}, u32[]{:S(2)}) copy-start(f32[784]{0:T(1024)S(1)} %fusion.57) | copy-start | bytes 9412
  129.7 114.9 %copy-start.47 = (f32[768]{0:T(1024)}, f32[768]{0:T(1024)S(1)}, u32[]{:S(2)}) copy-start(f32[768]{0:T(1024)S(1)} %mul.402) | copy-start | bytes 9220
  130.6 114.0 %copy-start.58 = (f32[768]{0:T(1024)}, f32[768]{0:T(1024)S(1)}, u32[]{:S(2)}) copy-start(f32[768]{0:T(1024)S(1)} %add.123) | copy-start | bytes 9220
  232.0 12.5 %copy-start.20 = (bf16[784,768]{1,0:T(8,128)(2,1)S(1)}, bf16[784,768]{1,0:T(8,128)(2,1)}, u32[]{:S(2)}) copy-start(bf16[784,768]{1,0:T(8,128)(2,1)} %param.17) | copy-start | bytes 3612676
  274.3 10.3 %copy-start.22 = (bf16[4,196,1,12,64]{1,4,3,0,2:T(8,128)(2,1)}, bf16[4,196,1,12,64]{1,4,3,0,2:T(8,128)(2,1)S(1)}, u32[]{:S(2)}) copy-start(bf16[4,196,1,12,64]{1,4,3,0,2:T(8,128)(2,1)S(1)} %copy.136) | copy-start | bytes 3612676
  298.2 32.6 %slice-start.9 = ((s8[4718592]{0:T(1024)(128)(4,1)}), s8[4194304]{0:T(1024)(128)(4,1)S(1)}, s32[]{:S(2)}) async-start(s8[4718592]{0:T(1024)(128)(4,1)} %bitcast.204), calls=%async_computation.9 | async-start | bytes 8388608
  301.3 29.4 %copy-start.25 = (f32[784,768]{1,0:T(8,128)}, f32[784,768]{1,0:T(8,128)S(1)}, u32[]{:S(2)}) copy-start(f32[784,768]{1,0:T(8,128)S(1)} %get-tuple-element.107) | copy-start | bytes 7225348
  302.7 28.0 %slice-start.10 = ((s8[4718592]{0:T(1024)(128)(4,1)}), s8[524288]{0:T(1024)(128)(4,1)S(1)}, s32[]{:S(2)}) async-start(s8[4718592]{0:T(1024)(128)(4,1)} %bitcast.204), calls=%async_computation.10 | async-start | bytes 1048576
  342.9 61.9 %copy-start.60 = (s32[512]{0:T(512)S(1)}, s32[512]{0:T(512)}, u32[]{:S(2)}) copy-start(s32[512]{0:T(512)} %param.19) | copy-start | bytes 6148
  433.1 13.9 %slice-start.7 = ((s8[4718592]{0:T(1024)(128)(4,1)}), s8[524288]{0:T(1024)(128)(4,1)S(1)}, s32[]{:S(2)}) async-start(s8[4718592]{0:T(1024)(128)(4,1)} %bitcast.202), calls=%async_computation.7 | async-start | bytes 1048576
  434.2 12.8 %copy-start.26 = (f32[784,768]{1,0:T(8,128)S(1)}, f32[784,768]{1,0:T(8,128)}, u32[]{:S(2)}) copy-start(f32[784,768]{1,0:T(8,128)} %copy-done.25) | copy-start | bytes 7225348
  434.3 12.8 %slice-start.8 = ((s8[4718592]{0:T(1024)(128)(4,1)}), s8[4194304]{0:T(1024)(128)(4,1)S(1)}, s32[]{:S(2)}) async-start(s8[4718592]{0:T(1024)(128)(4,1)} %bitcast.202), calls=%async_computation.8 | async-start | bytes 8388608
  462.2 9.7 %copy-start.54 = (f32[784]{0:T(1024)S(1)}, f32[784]{0:T(1024)}, u32[]{:S(2)}) copy-start(f32[784]{0:T(1024)} %copy-done.53) | copy-start | bytes 9412
  506.1 12.9 %slice-start.5 = ((s8[6291456]{0:T(1024)(128)(4,1)}), s8[2097152]{0:T(1024)(128)(4,1)S(1)}, s32[]{:S(2)}) async-start(s8[6291456]{0:T(1024)(128)(4,1)} %bitcast.189), calls=%async_computation.5 | async-start | bytes 4194304
  534.1 15.4 %slice-start = ((s8[9830400]{0:T(1024)(128)(4,1)}), s8[4194304]{0:T(1024)(128)(4,1)S(1)}, s32[]{:S(2)}) async-start(s8[9830400]{0:T(1024)(128)(4,1)} %bitcast.184), calls=%async_computation | async-start | bytes 8388608
  534.1 15.4 %slice-start.1 = ((s8[9830400]{0:T(1024)(128)(4,1)}), s8[4194304]{0:T(1024)(128)(4,1)S(1)}, s32[]{:S(2)}) async-start(s8[9830400]{0:T(1024)(128)(4,1)} %bitcast.184), calls=%async_computation.1 | async-start | bytes 8388608
  556.4 11.9 %copy-start.23 = (bf16[4,196,1,12,64]{1,4,3,0,2:T(8,128)(2,1)S(1)}, bf16[4,196,1,12,64]{1,4,3,0,2:T(8,128)(2,1)}, u32[]{:S(2)}) copy-start(bf16[4,196,1,12,64]{1,4,3,0,2:T(8,128)(2,1)} %copy-done.22) | copy-start | bytes 3612676
  (54 other events, 198.4 us)
